TPU v7x, 128 devices: a whole 4x4x4 slice. The times are simulated.
128 devices in a mesh: face: 4 (over y), blk: 32 (over z, x, core).
Axes of the slice: x: 4, y: 4, z: 4, core: 2. Of those that a mesh axis runs over, the one named last changes fastest.
Arguments:
- field: bfloat16 [8192, 64, 128], P(('face', 'blk')), may hold values from -6 to 6
- patch_rows: int32 [384, 64], P(('face', 'blk')), may hold values from 0 to 8191, as said below
- flips: int32 [384, 64], P(('face', 'blk')), may hold values from 0 to 1, as said below
- blend_weights: int32 [384, 64, 64], P(('face', 'blk')), may hold values from 1 to 8
- live: int32 [128], P(('face', 'blk')), may hold values from 2 to 3, as said below
- kernel_one: bfloat16 [3, 3, 128, 128], replicated, may hold values from -0.1875 to 0.1875
- bias_one: float32 [128], replicated, may hold values from -3 to 3
- kernel_two: bfloat16 [3, 3, 128, 128], replicated, may hold values from -0.1875 to 0.1875
- bias_two: float32 [128], replicated, may hold values from -3 to 3
Outputs:
- blended: bfloat16 [8192, 64, 128], P(('face', 'blk'))
Inputs may be any that keep to these rules, and one draw needn't show every extreme that they name: `patch_rows`: device d's slots list 64 consecutive rows modulo 8192 each, starting between d * 64 - 32 and (d + 1) * 64 - 32; reads reach exactly 32 rows beyond device 0's rows on both sides; every row is read by some live slot; slots that are not live hold valid rows and are ignored. `flips`: 1 exactly where the row lies in another face group than the slot's device. Device 0 has all 3 slots live.
All inputs are finite; a program needn't handle non-finite values.
Results may differ from a plain program's by a relative error of at most 0.006.
Values may be sent and summed in bfloat16 or wider, within the bound.
A program may use at most 192 MiB of HBM per device.

v0:
```python
import functools

import jax
import jax.numpy as jnp
from jax import lax
from jax.experimental import pallas as pl
from jax.experimental.pallas import tpu as pltpu
from jax.sharding import PartitionSpec as P

MESH = pl.DeviceIdType.MESH
F32, BF16, I32 = jnp.float32, jnp.bfloat16, jnp.int32
SIDE, C, RIM, SLOTS = 64, 128, 32, 3
LINE = 8
X_ZERO = 68
H_ZERO = 66
H_EDGE = 67
N_EDGE = 12
N_ROWS = 18


def shifts(rows):
    column = lax.broadcasted_iota(I32, rows.shape, 1)
    left = jnp.where(column == 0, 0.0, pltpu.roll(rows, 1, 1))
    right = jnp.where(column == SIDE - 1, 0.0, pltpu.roll(rows, SIDE - 1, 1))
    return left, rows, right


def pair_rows(rows):
    n = rows.shape[0] // 2
    rows = rows.reshape(n, 2, SIDE, C)
    return jnp.concatenate([rows[:, 0], rows[:, 1]], axis=-1).reshape(n * SIDE, 2 * C)


def pair_dot(parts, w_ref, conv):
    lhs = jnp.concatenate([parts[t][p] for t in range(3) for p in range(2)], axis=-1)
    rhs = jnp.concatenate(
        [w_ref[conv, 2 * p : 2 * p + 2, t].reshape(2 * C, 2 * C) for t in range(3) for p in range(2)], axis=0
    )
    return jnp.dot(lhs, rhs, preferred_element_type=F32)


def unpair(wide):
    n = wide.shape[0] // SIDE
    return jnp.stack(
        [wide[:, :C].reshape(n, SIDE, C), wide[:, C:].reshape(n, SIDE, C)], axis=1
    )


def silu(z):
    return z * (0.5 + 0.5 * jnp.tanh(0.5 * z))


def work(
    faces, blks,
    field, rows, live, weights, k_one, k_two, b_one, b_two,
    base_out, edge_out, index_out,
    x3, h3, r_main, r_turn, wmat, wts, w_send, rim_in, w_in, rows_in, wown, wnear, cov, inside, base, edge, index,
    rows_s, live_s,
    field_sem, load_sem, send_sem, recv_sem, out_sem,
):
    me_face, me_blk = lax.axis_index("face"), lax.axis_index("blk")
    total = faces * blks
    me = me_face * blks + me_blk
    following = lax.rem(me + 1, total)
    preceding = lax.rem(me + total - 1, total)
    after = (following // blks, lax.rem(following, blks))
    before = (preceding // blks, lax.rem(preceding, blks))
    first = jnp.where(me_blk == 0, 1, 0)
    last = jnp.where(me_blk == blks - 1, 1, 0)
    boundary = jnp.logical_or(me_blk == 0, me_blk == blks - 1)
    n_total = total * SIDE

    barrier = pltpu.get_barrier_semaphore()
    for other in (after, before):
        pl.semaphore_signal(barrier, inc=1, device_id=other, device_id_type=MESH)

    small_loads = [
        pltpu.make_async_copy(live, live_s, load_sem.at[5]),
        pltpu.make_async_copy(rows, rows_s, load_sem.at[6]),
        pltpu.make_async_copy(weights, wts, load_sem.at[0]),
    ]
    for c in small_loads:
        c.start()
    field_loads = [
        pltpu.make_async_copy(field.at[pl.ds(16 * n, 16)], x3.at[1, pl.ds(2 + 16 * n, 16)], field_sem.at[n])
        for n in range(4)
    ]
    kernel_loads = [
        pltpu.make_async_copy(
            src, wmat.at[conv, pl.ds(q, 3), :, :, pl.ds(q * C, C)], load_sem.at[1 + 2 * conv + q]
        )
        for conv, src in enumerate((k_one, k_two)) for q in range(2)
    ]
    for c in field_loads[:2] + kernel_loads[:2] + field_loads[2:] + kernel_loads[2:]:
        c.start()

    for conv in range(2):
        wmat[conv, 0, :, :, C:] = jnp.zeros((3, C, C), BF16)
        wmat[conv, 3, :, :, :C] = jnp.zeros((3, C, C), BF16)
    for t in range(3):
        x3[t, X_ZERO] = jnp.zeros((SIDE, C), BF16)
        h3[0, t, H_ZERO] = jnp.zeros((SIDE, C), BF16)
        h3[1, t, H_ZERO] = jnp.zeros((SIDE, C), BF16)
    wown[...] = jnp.zeros(wown.shape, F32)
    wnear[...] = jnp.zeros(wnear.shape, F32)

    def start_of(row, device):
        return jnp.minimum(lax.rem(row - device * SIDE + RIM + 2 * n_total, n_total), 2 * RIM) - RIM

    for c in small_loads:
        c.wait()
    for slot in range(SLOTS):
        own = jnp.where(slot < live_s[0], wts[slot], 0)
        w_send[slot] = own
        wown[slot, 64:128] = own.astype(F32)
    own_starts = [start_of(rows_s[p, 0], me) for p in range(SLOTS)]

    exchanges = []
    for n, (other, at, part) in enumerate(((after, SIDE - 2, RIM), (before, 0, 0))):
        exchanges.append([
            pltpu.make_async_remote_copy(
                src_ref=src, dst_ref=dst, send_sem=send_sem.at[n, m], recv_sem=recv_sem.at[n, m],
                device_id=other, device_id_type=MESH,
            )
            for m, (src, dst) in enumerate((
                (field.at[pl.ds(at, 2)], rim_in.at[n]),
                (w_send.at[:, pl.ds(part, RIM)], w_in.at[n]),
                (rows, rows_in.at[n]),
            ))
        ])

    def send():
        pl.semaphore_wait(barrier, 2)
        for n in range(2):
            for c in exchanges[n]:
                c.start()

    def shift_field(start, count):
        left, _, right = shifts(x3[1, start : start + count].astype(F32))
        x3[0, start : start + count] = left.astype(BF16)
        x3[2, start : start + count] = right.astype(BF16)

    def run_parts(src, first_row, pairs, mirrored):
        return [
            tuple(pair_rows(src[2 - t if mirrored else t, pl.ds(first_row + 2 * p, 2 * pairs)]) for p in range(2))
            for t in range(3)
        ]

    bias_one = b_one[...]
    bias_two = b_two[...]

    def hidden_of(acc):
        h = unpair(acc)
        h = silu(h.reshape(-1, SIDE, C) + bias_one.reshape(1, 1, C))
        return [v.astype(BF16) for v in shifts(h)]

    def first_conv(view, first_row, pairs, mirrored):
        made = hidden_of(pair_dot(run_parts(x3, first_row, pairs, mirrored), wmat, 0))
        for t in range(3):
            h3[view, t, pl.ds(first_row, 2 * pairs)] = made[t]

    def second_conv(view, pair, pairs, mirrored, dst):
        acc = pair_dot(run_parts(h3.at[view], 2 * pair, pairs, mirrored), wmat, 1)
        r = unpair(acc).reshape(2 * pairs, SIDE, C) + bias_two.reshape(1, 1, C)
        dst[pl.ds(2 * pair, 2 * pairs)] = r + x3[1, pl.ds(2 + 2 * pair, 2 * pairs)].astype(F32)

    field_loads[0].wait()
    shift_field(2, 16)
    line_start = lax.rem(me_blk, LINE) == 0
    pl.when(jnp.logical_not(line_start))(send)
    field_loads[1].wait()
    shift_field(18, 16)
    for c in kernel_loads[:2]:
        c.wait()
    first_conv(0, 2, 7, False)
    field_loads[2].wait()
    shift_field(34, 16)
    field_loads[3].wait()
    shift_field(50, 16)
    first_conv(0, 16, 8, False)
    first_conv(0, 32, 8, False)
    first_conv(0, 48, 8, False)
    for c in kernel_loads[2:]:
        c.wait()
    second_conv(0, 1, 8, False, r_main)
    second_conv(0, 9, 8, False, r_main)
    second_conv(0, 17, 8, False, r_main)
    second_conv(0, 25, 6, False, r_main)
    pl.when(jnp.logical_and(line_start, me > 0))(send)

    @pl.when(boundary)
    def _():
        b = jnp.where(me_blk == 0, 0, 15)
        first_conv(1, 2 * (1 + b), 8, True)
        first_conv(1, 2 * (9 + b), 8, True)
        second_conv(1, 1 + b, 8, True, r_turn)
        second_conv(1, 9 + b, 7, True, r_turn)

    def lanes(ref, r):
        return jnp.concatenate([ref(r[0]), ref(r[1])], axis=-1)

    def items_first(items):
        parts = [
            tuple(
                jnp.concatenate([
                    lanes(lambda i: x3[t + m * (2 - 2 * t), i], r[2 * p : 2 * p + 2]) for r, m in items
                ], axis=0)
                for p in range(2)
            )
            for t in range(3)
        ]
        return hidden_of(pair_dot(parts, wmat, 0))

    def items_second(items):
        parts = [
            tuple(
                jnp.concatenate([
                    lanes(lambda i: h3[v, t + m * (2 - 2 * t), i], r[2 * p : 2 * p + 2]) for v, r, m, _ in items
                ], axis=0)
                for p in range(2)
            )
            for t in range(3)
        ]
        r = unpair(pair_dot(parts, wmat, 1)) + bias_two.reshape(1, 1, 1, C)
        return [
            [r[n, q] + x3[1, residual[q]].astype(F32) for q in range(2)]
            for n, (_, _, _, residual) in enumerate(items)
        ]

    own_first, own_second, own_lead, own_weights = [], [], [], []
    for p in range(SLOTS):
        s = own_starts[p]
        e = s + SIDE - 1
        top = s > 0
        own_first.append((
            (jnp.where(top, X_ZERO, e + 1), jnp.where(top, s + 2, e + 2), jnp.where(top, s + 3, X_ZERO), X_ZERO), 0))
        own_second.append((
            0,
            (jnp.where(top, H_ZERO, e - 1), jnp.where(top, H_EDGE + p, e),
             jnp.where(top, s + 2, H_EDGE + p), jnp.where(top, s + 3, H_ZERO)),
            0,
            (jnp.where(top, s + 2, e + 1), jnp.where(top, s + 3, e + 2)),
        ))
        own_lead.append(jnp.where(top, s, e - 1))
        own_weights.append([jnp.where(top, wown[p, 64 + q : 65 + q], wown[p, 126 + q : 127 + q]) for q in range(2)])
    own_first.append(((X_ZERO, 2, 3, X_ZERO), 0))
    own_second.append((0, (H_ZERO, H_EDGE + 3, 2, 3), 0, (2, 3)))
    made = items_first(own_first)
    for t in range(3):
        for n in range(4):
            h3[0, t, H_EDGE + n] = made[t][2 * n]
    own_result = items_second(own_second)
    for n in range(3):
        for q in range(2):
            edge[2 * n + q] = own_result[n][q]
    for q in range(2):
        edge[N_ROWS + q] = own_result[3][q]

    cov[...] = sum(wown[p, pl.ds(64 - own_starts[p], SIDE)] for p in range(SLOTS))
    inner = lax.broadcasted_iota(I32, (SIDE, SIDE), 0)
    within = jnp.logical_and(inner >= 2, inner < SIDE - 2)
    for p in range(SLOTS):
        wown[p, 64:128] = jnp.where(within, wown[p, 64:128], 0.0)
    inside[...] = sum(wown[p, pl.ds(64 - own_starts[p], SIDE)] for p in range(SLOTS))

    def own_at(where, row):
        return sum(
            jnp.where(jnp.logical_and(own_starts[p] == where, p < live_s[0]), wts[p, row : row + 1], 0)
            for p in range(SLOTS)
        ).astype(F32)

    def spread(columns, n):
        return jnp.broadcast_to(columns[:, n : n + 1], (SIDE, C))

    def in_range(row):
        return jnp.logical_and(row >= 0, row < SIDE)

    def coefficients(pairs):
        made = [
            jnp.where(in_range(row), w / cov[pl.ds(jnp.clip(row, 0, SIDE - 1), 1)], 0.0) for w, row in pairs
        ]
        made += [jnp.zeros((1, SIDE), F32)] * (-len(made) % 8)
        return jnp.concatenate(made, axis=0).T

    pl.when(me == 0)(send)

    row_i = lax.broadcasted_iota(I32, (SIDE, SIDE), 0)
    col_i = lax.broadcasted_iota(I32, (SIDE, SIDE), 1)
    indices = [None] * N_ROWS
    writes = []

    def side_of(n):
        flag = (first, last)[n]
        for c in exchanges[n]:
            c.wait_recv()
        turn = jnp.where(flag == 1, SIDE - 1 - col_i, col_i)
        turn = jnp.where(row_i == turn, 1.0, 0.0).astype(BF16)
        rim = jnp.dot(turn, jnp.concatenate([rim_in[n, 0], rim_in[n, 1]], axis=-1), preferred_element_type=F32)
        rim = jnp.stack([rim[:, :C], rim[:, C:]], axis=0)
        for t, v in enumerate(shifts(rim)):
            x3[t, (0, 66)[n] : (2, 68)[n]] = v.astype(BF16)
        starts = [
            start_of(rows_in[n, p, 0], me - 1 if n == 0 else me + 1) + (-SIDE, SIDE)[n] for p in range(SLOTS)
        ]
        pair_first, pair_second = (0, 32)[n], (0, 31)[n]
        items = [
            (tuple(2 * pair_first + j for j in range(4)), 0),
            (tuple(2 * pair_first + j for j in range(4)), flag),
            ((X_ZERO, 1, 2, X_ZERO) if n == 0 else (65, 66, X_ZERO, X_ZERO), 0),
        ]
        static = H_EDGE + 4 + n
        tails = [
            (0, tuple(2 * pair_second + j for j in range(4)), 0, (2 * pair_second + 2, 2 * pair_second + 3)),
            (flag, tuple(2 * pair_second + j for j in range(4)), flag, (2 * pair_second + 2, 2 * pair_second + 3)),
            (0, (H_ZERO, static, 1, 2), 0, (1, 2)) if n == 0 else (0, (63, 64, static, H_ZERO), 0, (65, 66)),
        ]
        for p in range(SLOTS):
            at = H_EDGE + 6 + 3 * n + p
            if n == 0:
                e = jnp.clip(starts[p] + SIDE - 1, 0, RIM - 1)
                items.append(((e + 1, e + 2, X_ZERO, X_ZERO), flag))
                tails.append((flag, (jnp.maximum(e - 1, 0), e, at, H_ZERO), flag, (e + 1, e + 2)))
            else:
                s = jnp.clip(starts[p], RIM, SIDE - 1)
                items.append(((X_ZERO, s + 2, s + 3, X_ZERO), flag))
                tails.append((flag, (H_ZERO, at, s + 2, s + 3), flag, (s + 2, s + 3)))
        made = items_first(items)
        for t in range(3):
            h3[flag, t, 2 * pair_first : 2 * pair_first + 2] = made[t][2:4]
            h3[0, t, 2 * pair_first : 2 * pair_first + 2] = made[t][0:2]
            h3[0, t, static] = made[t][4]
            for p in range(SLOTS):
                h3[flag, t, H_EDGE + 6 + 3 * n + p] = made[t][6 + 2 * p]
        result = items_second(tails)

        w = jnp.dot(
            w_in[n].reshape(SLOTS * RIM, SIDE).astype(F32).astype(BF16), turn, preferred_element_type=F32
        ).reshape(SLOTS, RIM, SIDE)
        inner = lax.broadcasted_iota(I32, w.shape, 1)
        w_inside = jnp.where(inner < RIM - 2, w, 0.0) if n == 0 else jnp.where(inner >= 2, w, 0.0)
        home = (0, 64)[n]
        half = (0, RIM)[n]
        wnear[n, 0, :, home : home + RIM] = w
        wnear[n, 1, :, home : home + RIM] = w_inside
        offsets = [-RIM - starts[p] if n == 0 else 3 * RIM - starts[p] for p in range(SLOTS)]
        cover, near = [
            sum(wnear[n, i, p, pl.ds(offsets[p], RIM)] for p in range(SLOTS)) for i in range(2)
        ]
        cover = cover + cov[half : half + RIM]
        cov[half : half + RIM] = cover
        flag_f = flag.astype(F32)
        plain = (inside[half : half + RIM] + (1.0 - flag_f) * near) / cover
        turned = flag_f * near / cover
        both = jnp.concatenate([plain, turned], axis=0).T

        pairs = []
        for p in range(SLOTS):
            lead = starts[p] + SIDE - 2 if n == 0 else starts[p]
            for q in range(2):
                own_row = RIM - 2 + q if n == 0 else q
                pairs.append((w[p, own_row : own_row + 1], lead + q))
                indices[6 + 6 * n + 2 * p + q] = jnp.clip(lead + q, 0, SIDE - 1)
        if n == 0:
            pairs += [(own_at(-1, 1), 0), (own_at(0, 0), 0), (own_at(0, 1), 1)]
            for p in range(SLOTS):
                for q in range(2):
                    pairs.append((own_weights[p][q], own_lead[p] + q))
                    indices[2 * p + q] = jnp.clip(own_lead[p] + q, 0, SIDE - 1)
        else:
            pairs.append((own_at(1, SIDE - 2), SIDE - 1))
        columns = coefficients(pairs)
        for p in range(SLOTS):
            for q in range(2):
                edge[6 + 6 * n + 2 * p + q] = result[3 + p][q] * spread(columns, 2 * p + q)
        if n == 0:
            for k in range(6):
                edge[k] = edge[k] * spread(columns, 9 + k)
            lane = lax.broadcasted_iota(I32, (8, C), 1)
            packed = jnp.zeros((8, C), I32)
            for k in range(N_ROWS):
                packed = jnp.where(lane == k, indices[k], packed)
            index[...] = packed
            writes.append(pltpu.make_async_copy(edge.at[pl.ds(0, N_ROWS)], edge_out, out_sem.at[0]))
            writes.append(pltpu.make_async_copy(index, index_out, out_sem.at[1]))
            for c in writes[-2:]:
                c.start()
        r_main[2 * pair_second] = result[0][0]
        r_main[2 * pair_second + 1] = result[0][1]
        r_turn[2 * pair_second] = result[1][0]
        r_turn[2 * pair_second + 1] = result[1][1]

        def extra(r):
            if n == 0 and r == 0:
                return result[2][1] * spread(columns, 6) + edge[N_ROWS] * spread(columns, 7)
            if n == 0 and r == 1:
                return edge[N_ROWS + 1] * spread(columns, 8)
            if n == 1 and r == SIDE - 1:
                return result[2][0] * spread(columns, 6)
            return 0.0

        r_extra = {r: extra(r) for r in (0, 1, SIDE - 1) if half <= r < half + RIM}
        for r, v in r_extra.items():
            cov_row = v
            edge[N_ROWS + 2 + (r if r < 2 else 0)] = cov_row

        def fill(turned_too):
            for r in range(half, half + RIM):
                v = r_main[r] * spread(both, r - half)
                if turned_too:
                    v = v + r_turn[r] * spread(both, RIM + r - half)
                if r in r_extra:
                    v = v + edge[N_ROWS + 2 + (r if r < 2 else 0)]
                base[r] = v.astype(BF16)

        pl.when(flag == 0)(functools.partial(fill, False))
        pl.when(flag == 1)(functools.partial(fill, True))
        c = pltpu.make_async_copy(base.at[pl.ds(half, RIM)], base_out.at[pl.ds(half, RIM)], out_sem.at[2 + n])
        c.start()
        writes.append(c)

    side_of(1)
    side_of(0)
    for n in range(2):
        for c in exchanges[n]:
            c.wait_send()
    for c in writes:
        c.wait()


def place(index, base, edge, out, index_s, base_v, edge_v, acc, load_sem, out_sem):
    loads = [
        pltpu.make_async_copy(index, index_s, load_sem.at[0]),
        pltpu.make_async_copy(edge, edge_v, load_sem.at[1]),
        pltpu.make_async_copy(base, base_v, load_sem.at[2]),
    ]
    for c in loads:
        c.start()
    for c in loads:
        c.wait()
    rows = [index_s[0, n] for n in range(N_ROWS)]
    for n in range(N_ROWS):
        acc[rows[n]] = base_v[rows[n]].astype(F32)
    for n in range(N_ROWS):
        acc[rows[n]] += edge_v[n]
    for n in range(N_ROWS):
        base_v[rows[n]] = acc[rows[n]].astype(BF16)
    store = pltpu.make_async_copy(base_v, out, out_sem)
    store.start()
    store.wait()


def shards(field, patch_rows, flips, blend_weights, live, kernel_one, bias_one, kernel_two, bias_two):
    faces, blks = lax.axis_size("face"), lax.axis_size("blk")
    anywhere = pl.BlockSpec(memory_space=pl.ANY)
    vectors = pl.BlockSpec(memory_space=pltpu.VMEM)
    base, edge, index = pl.pallas_call(
        functools.partial(work, faces, blks),
        out_shape=(
            jax.ShapeDtypeStruct((SIDE, SIDE, C), BF16),
            jax.ShapeDtypeStruct((N_ROWS, SIDE, C), F32),
            jax.ShapeDtypeStruct((8, C), I32),
        ),
        in_specs=[anywhere] * 6 + [vectors] * 2,
        out_specs=(anywhere,) * 3,
        scratch_shapes=[
            pltpu.VMEM((3, X_ZERO + 1, SIDE, C), BF16),
            pltpu.VMEM((2, 3, H_EDGE + N_EDGE, SIDE, C), BF16),
            pltpu.VMEM((SIDE, SIDE, C), F32),
            pltpu.VMEM((SIDE, SIDE, C), F32),
            pltpu.VMEM((2, 4, 3, C, 2 * C), BF16),
            pltpu.VMEM((SLOTS, SIDE, SIDE), I32),
            pltpu.VMEM((SLOTS, SIDE, SIDE), I32),
            pltpu.VMEM((2, 2, SIDE, C), BF16),
            pltpu.VMEM((2, SLOTS, RIM, SIDE), I32),
            pltpu.VMEM((2, SLOTS, SIDE), I32),
            pltpu.VMEM((SLOTS, 192, SIDE), F32),
            pltpu.VMEM((2, 2, SLOTS, 96, SIDE), F32),
            pltpu.VMEM((SIDE, SIDE), F32),
            pltpu.VMEM((SIDE, SIDE), F32),
            pltpu.VMEM((SIDE, SIDE, C), BF16),
            pltpu.VMEM((N_ROWS + 4, SIDE, C), F32),
            pltpu.VMEM((8, C), I32),
            pltpu.SMEM((SLOTS, SIDE), I32),
            pltpu.SMEM((1,), I32),
            pltpu.SemaphoreType.DMA((4,)),
            pltpu.SemaphoreType.DMA((7,)),
            pltpu.SemaphoreType.DMA((2, 3)),
            pltpu.SemaphoreType.DMA((2, 3)),
            pltpu.SemaphoreType.DMA((4,)),
        ],
        compiler_params=pltpu.CompilerParams(
            collective_id=0, has_side_effects=True, vmem_limit_bytes=62 * 2**20
        ),
    )(
        field, patch_rows, live, blend_weights, kernel_one, kernel_two,
        bias_one.reshape(1, C), bias_two.reshape(1, C),
    )
    return pl.pallas_call(
        place,
        out_shape=jax.ShapeDtypeStruct((SIDE, SIDE, C), BF16),
        in_specs=[anywhere] * 3,
        out_specs=anywhere,
        scratch_shapes=[
            pltpu.SMEM((8, C), I32),
            pltpu.VMEM((SIDE, SIDE, C), BF16),
            pltpu.VMEM((N_ROWS, SIDE, C), F32),
            pltpu.VMEM((SIDE, SIDE, C), F32),
            pltpu.SemaphoreType.DMA((3,)),
            pltpu.SemaphoreType.DMA,
        ],
        compiler_params=pltpu.CompilerParams(vmem_limit_bytes=62 * 2**20),
    )(index, base, edge)


def solution(mesh):
    split = ("face", "blk")
    placed = (P(split, None, None), P(split, None), P(split, None), P(split, None, None), P(split), P(), P(), P(), P())
    return jax.shard_map(shards, mesh=mesh, in_specs=placed, out_specs=P(split, None, None), check_vma=False)
```

profile of v0, /device:TPU:127, one launch (start us, length us, event | category | flops | bytes accessed | tf_op | source)
XLA Modules:
  0.0 20.1 jit_solution(8709810922549599964)
XLA Ops:
  0.7 16.9 %shard_map.82 = (bf16[64,64,128]{2,1,0:T(8,128)(2,1)}, f32[18,64,128]{2,1,0:T(8,128)}, s32[8,128]{1,0:T(8,128)}) custom-call(bf16[64,64,128]{2,1,0:T(8,128)(2,1)} %field.1, s32[3,64]{1,0:T(4,128)} %rows.1, s32[1]{0:T(128)S(6)} %copy.9.live, s32[3,64,64]{2,1,0:T(8,128)} %weights.1, bf16[3,3,128,128]{3,2,1,0:T(8,128)(2,1)} %k_one.1, ...), custom_call_target="tpu_custom_call" | custom-call | tf_op jit(solution)/shard_map/pallas_call | solution.py:456
  17.6 2.6 %shard_map.83 = bf16[64,64,128]{2,1,0:T(8,128)(2,1)} custom-call(s32[8,128]{1,0:T(8,128)} %get-tuple-element.8.index, bf16[64,64,128]{2,1,0:T(8,128)(2,1)} %get-tuple-element.9.base, f32[18,64,128]{2,1,0:T(8,128)} %get-tuple-element.10.edge), custom_call_target="tpu_custom_call" | custom-call | tf_op jit(solution)/shard_map/pallas_call | solution.py:498
where the time goes:
time: 20.3 us; the launch traced here: 20.1 us
  Pallas kernels  19.5 us (96%)
  between operations  0.66 us (3%)
    pallas_call x1, Pallas kernels, shards(): pl.pallas_call(functools.partial(work, faces, blks), out_shape=(jax.Shape...  16.9 us
    pallas_call x1, Pallas kernels, shards(): pl.pallas_call(place, out_shape=jax.ShapeDtypeStruct((SIDE, SIDE, C), BF1...  2.57 us

commit v1 on v0

v1 whole, which is shorter than its diff:
```python
import functools

import jax
import jax.numpy as jnp
from jax import lax
from jax.experimental import pallas as pl
from jax.experimental.pallas import tpu as pltpu
from jax.sharding import PartitionSpec as P

MESH = pl.DeviceIdType.MESH
F32, BF16, I32 = jnp.float32, jnp.bfloat16, jnp.int32
SIDE, C, RIM, SLOTS = 64, 128, 32, 3
X_ZERO = 68
H_ZERO = 66
H_EDGE = 67
N_EDGE = 12
N_ROWS = 18


def shifts(rows):
    column = lax.broadcasted_iota(I32, rows.shape, 1)
    left = jnp.where(column == 0, 0.0, pltpu.roll(rows, 1, 1))
    right = jnp.where(column == SIDE - 1, 0.0, pltpu.roll(rows, SIDE - 1, 1))
    return left, rows, right


def pair_rows(rows):
    n = rows.shape[0] // 2
    rows = rows.reshape(n, 2, SIDE, C)
    return jnp.concatenate([rows[:, 0], rows[:, 1]], axis=-1).reshape(n * SIDE, 2 * C)


def pair_dot(parts, w_ref, conv):
    lhs = jnp.concatenate([parts[t][p] for t in range(3) for p in range(2)], axis=-1)
    rhs = jnp.concatenate(
        [w_ref[conv, 2 * p : 2 * p + 2, t].reshape(2 * C, 2 * C) for t in range(3) for p in range(2)], axis=0
    )
    return jnp.dot(lhs, rhs, preferred_element_type=F32)


def unpair(wide):
    n = wide.shape[0] // SIDE
    return jnp.stack(
        [wide[:, :C].reshape(n, SIDE, C), wide[:, C:].reshape(n, SIDE, C)], axis=1
    )


def silu(z):
    return z * (0.5 + 0.5 * jnp.tanh(0.5 * z))


def work(
    faces, blks,
    field, rows, live, weights, k_one, k_two, b_one, b_two,
    base_out, edge_out, index_out,
    x3, h3, r_all, wmat, wts, w_send, w_in, rim, rim_in, rows_in, wown, cov, base, blend, own_rows, edge, index,
    rows_s, live_s,
    field_sem, load_sem, send_sem, recv_sem, out_sem,
):
    me_face, me_blk = lax.axis_index("face"), lax.axis_index("blk")
    total = faces * blks
    me = me_face * blks + me_blk
    following = lax.rem(me + 1, total)
    preceding = lax.rem(me + total - 1, total)
    after = (following // blks, lax.rem(following, blks))
    before = (preceding // blks, lax.rem(preceding, blks))
    first = jnp.where(me_blk == 0, 1, 0)
    last = jnp.where(me_blk == blks - 1, 1, 0)
    boundary = jnp.logical_or(me_blk == 0, me_blk == blks - 1)
    n_total = total * SIDE

    barrier = pltpu.get_barrier_semaphore()
    for other in (after, before):
        pl.semaphore_signal(barrier, inc=1, device_id=other, device_id_type=MESH)

    small_loads = [
        pltpu.make_async_copy(live, live_s, load_sem.at[5]),
        pltpu.make_async_copy(rows, rows_s, load_sem.at[6]),
        pltpu.make_async_copy(weights, wts, load_sem.at[0]),
        pltpu.make_async_copy(field.at[pl.ds(SIDE - 2, 2)], rim.at[2, pl.ds(0, 2)], load_sem.at[7]),
        pltpu.make_async_copy(field.at[pl.ds(0, 2)], rim.at[2, pl.ds(2, 2)], load_sem.at[8]),
    ]
    field_loads = [
        pltpu.make_async_copy(field.at[pl.ds(16 * n, 16)], x3.at[1, pl.ds(2 + 16 * n, 16)], field_sem.at[n])
        for n in range(4)
    ]
    kernel_loads = [
        pltpu.make_async_copy(
            src, wmat.at[conv, pl.ds(q, 3), :, :, pl.ds(q * C, C)], load_sem.at[1 + 2 * conv + q]
        )
        for conv, src in enumerate((k_one, k_two)) for q in range(2)
    ]
    for c in small_loads + field_loads[:1] + kernel_loads[:2] + field_loads[1:] + kernel_loads[2:]:
        c.start()

    for conv in range(2):
        wmat[conv, 0, :, :, C:] = jnp.zeros((3, C, C), BF16)
        wmat[conv, 3, :, :, :C] = jnp.zeros((3, C, C), BF16)
    for t in range(3):
        x3[t, X_ZERO] = jnp.zeros((SIDE, C), BF16)
        h3[0, t, H_ZERO] = jnp.zeros((SIDE, C), BF16)
        h3[1, t, H_ZERO] = jnp.zeros((SIDE, C), BF16)
    wown[...] = jnp.zeros(wown.shape, F32)

    def start_of(row, device):
        return jnp.minimum(lax.rem(row - device * SIDE + RIM + 2 * n_total, n_total), 2 * RIM) - RIM

    row_i = lax.broadcasted_iota(I32, (SIDE, SIDE), 0)
    col_i = lax.broadcasted_iota(I32, (SIDE, SIDE), 1)

    def prepare(to):
        for slot in range(SLOTS):
            wown[slot, 64:128] = jnp.where(slot < live_s[0], wts[slot], 0).astype(F32)
        for n, flag in enumerate((last, first)):
            turn = jnp.where(flag == 1, SIDE - 1 - col_i, col_i)
            turn = jnp.where(row_i == turn, 1.0, 0.0).astype(BF16)
            pair = jnp.concatenate([rim[2, 2 * n], rim[2, 2 * n + 1]], axis=-1)
            pair = jnp.dot(turn, pair, preferred_element_type=F32).astype(BF16)
            for i in range(2):
                rim[to, 2 * n + i] = pair[:, i * C : i * C + C]
            row = (128, 32)[n]
            line = (126, 64)[n]
            mine = jnp.concatenate(
                [sum(wown[p, pl.ds(row - start_of(rows_s[p, 0], me), RIM)] for p in range(SLOTS))]
                + [wown[p, line : line + 2] for p in range(SLOTS)] + [jnp.zeros((2, SIDE), F32)], axis=0)
            w_send[to, n] = jnp.dot(mine.astype(BF16), turn, preferred_element_type=F32)

    def exchange(n, at):
        return [
            pltpu.make_async_remote_copy(
                src_ref=src, dst_ref=dst, send_sem=send_sem.at[n, m], recv_sem=recv_sem.at[n, m],
                device_id=(after, before)[n], device_id_type=MESH,
            )
            for m, (src, dst) in enumerate((
                (rim.at[at, pl.ds(2 * n, 2)], rim_in.at[n]),
                (w_send.at[at, n], w_in.at[n]),
                (rows, rows_in.at[n]),
            ))
        ]

    exchanges = [exchange(n, 0) for n in range(2)]

    def send(at):
        pl.semaphore_wait(barrier, 2)
        for n in range(2):
            for c in exchange(n, at):
                c.start()

    def shift_field(start, count):
        left, _, right = shifts(x3[1, start : start + count].astype(F32))
        x3[0, start : start + count] = left.astype(BF16)
        x3[2, start : start + count] = right.astype(BF16)

    def stage(body):
        pl.when(me >= 0)(body)

    def run_parts(src, first_row, pairs, mirrored):
        return [
            tuple(pair_rows(src[2 - t if mirrored else t, pl.ds(first_row + 2 * p, 2 * pairs)]) for p in range(2))
            for t in range(3)
        ]

    bias_one = b_one[...]
    bias_two = b_two[...]

    def hidden_of(acc):
        h = unpair(acc)
        h = silu(h.reshape(-1, SIDE, C) + bias_one.reshape(1, 1, C))
        return [v.astype(BF16) for v in shifts(h)]

    def first_conv(view, first_row, pairs, mirrored):
        made = hidden_of(pair_dot(run_parts(x3, first_row, pairs, mirrored), wmat, 0))
        for t in range(3):
            h3[view, t, pl.ds(first_row, 2 * pairs)] = made[t]

    def second_conv(view, pair, pairs, mirrored):
        acc = pair_dot(run_parts(h3.at[view], 2 * pair, pairs, mirrored), wmat, 1)
        r = unpair(acc).reshape(2 * pairs, SIDE, C) + bias_two.reshape(1, 1, C)
        r = r + x3[1, pl.ds(2 + 2 * pair, 2 * pairs)].astype(F32)
        r_all[view, pl.ds(2 * pair, 2 * pairs)] = r
        if view == 0:
            base[pl.ds(2 * pair, 2 * pairs)] = r.astype(BF16)

    @pl.when(me_blk == blks - 1)
    def _():
        for c in small_loads:
            c.wait()
        prepare(0)
        send(0)

    field_loads[0].wait()
    shift_field(2, 16)
    for c in kernel_loads[:2]:
        c.wait()
    first_conv(0, 2, 7, False)

    @pl.when(me_blk < blks - 1)
    def _():
        for c in small_loads:
            c.wait()

    for c in field_loads[1:]:
        c.wait()

    @stage
    def _():
        shift_field(18, 48)
        first_conv(0, 16, 8, False)
        prepare(1)

    pl.when(jnp.logical_and(me_blk > 0, me_blk < blks - 1))(lambda: send(1))

    @stage
    def _():
        first_conv(0, 32, 8, False)
        first_conv(0, 48, 8, False)

    for c in kernel_loads[2:]:
        c.wait()

    @stage
    def _():
        second_conv(0, 1, 8, False)
        second_conv(0, 9, 8, False)
        second_conv(0, 17, 8, False)
        second_conv(0, 25, 6, False)

    writes = []
    for n, flag in enumerate((first, last)):
        bulk = pl.ds((2, RIM)[n], RIM - 2)
        writes.append(pltpu.make_async_copy(base.at[bulk], base_out.at[bulk], out_sem.at[2 + n]))
        pl.when(flag == 0)(writes[n].start)
    pl.when(jnp.logical_and(me_blk == 0, me > 0))(lambda: send(1))

    @pl.when(boundary)
    def _():
        b = jnp.where(me_blk == 0, 0, 15)
        first_conv(1, 2 * (1 + b), 8, True)
        first_conv(1, 2 * (9 + b), 8, True)

    pl.when(me == 0)(lambda: send(1))

    @pl.when(boundary)
    def _():
        b = jnp.where(me_blk == 0, 0, 15)
        second_conv(1, 1 + b, 8, True)
        second_conv(1, 9 + b, 7, True)

    own_starts = [start_of(rows_s[p, 0], me) for p in range(SLOTS)]

    def lanes(ref, r):
        return jnp.concatenate([ref(r[0]), ref(r[1])], axis=-1)

    def items_first(items):
        parts = [
            tuple(
                jnp.concatenate([
                    lanes(lambda i: x3[t + m * (2 - 2 * t), i], r[2 * p : 2 * p + 2]) for r, m in items
                ], axis=0)
                for p in range(2)
            )
            for t in range(3)
        ]
        return hidden_of(pair_dot(parts, wmat, 0))

    def items_second(items):
        parts = [
            tuple(
                jnp.concatenate([
                    lanes(lambda i: h3[v, t + m * (2 - 2 * t), i], r[2 * p : 2 * p + 2]) for v, r, m, _ in items
                ], axis=0)
                for p in range(2)
            )
            for t in range(3)
        ]
        r = unpair(pair_dot(parts, wmat, 1)) + bias_two.reshape(1, 1, 1, C)
        return [
            [r[n, q] + x3[1, residual[q]].astype(F32) for q in range(2)]
            for n, (_, _, _, residual) in enumerate(items)
        ]

    own_first, own_second, own_lead, own_weights = [], [], [], []
    for p in range(SLOTS):
        s = own_starts[p]
        e = s + SIDE - 1
        top = s > 0
        own_first.append((
            (jnp.where(top, X_ZERO, e + 1), jnp.where(top, s + 2, e + 2), jnp.where(top, s + 3, X_ZERO), X_ZERO), 0))
        own_second.append((
            0,
            (jnp.where(top, H_ZERO, e - 1), jnp.where(top, H_EDGE + p, e),
             jnp.where(top, s + 2, H_EDGE + p), jnp.where(top, s + 3, H_ZERO)),
            0,
            (jnp.where(top, s + 2, e + 1), jnp.where(top, s + 3, e + 2)),
        ))
        own_lead.append(jnp.where(top, s, e - 1))
        own_weights.append([jnp.where(top, wown[p, 64 + q : 65 + q], wown[p, 126 + q : 127 + q]) for q in range(2)])
    own_first.append(((X_ZERO, 2, 3, X_ZERO), 0))
    own_second.append((0, (H_ZERO, H_EDGE + 3, 2, 3), 0, (2, 3)))

    @stage
    def _():
        made = items_first(own_first)
        for t in range(3):
            for n in range(4):
                h3[0, t, H_EDGE + n] = made[t][2 * n]

    @stage
    def _():
        own_result = items_second(own_second)
        for n in range(4):
            for q in range(2):
                own_rows[2 * n + q] = own_result[n][q]

    cov[...] = sum(wown[p, pl.ds(64 - own_starts[p], SIDE)] for p in range(SLOTS))

    def own_at(where, row):
        return sum(
            jnp.where(jnp.logical_and(own_starts[p] == where, p < live_s[0]), wts[p, row : row + 1], 0)
            for p in range(SLOTS)
        ).astype(F32)

    def spread(columns, n):
        return jnp.broadcast_to(columns[:, n : n + 1], (SIDE, C))

    def in_range(row):
        return jnp.logical_and(row >= 0, row < SIDE)

    def coefficients(pairs):
        made = [
            jnp.where(in_range(row), w / cov[pl.ds(jnp.clip(row, 0, SIDE - 1), 1)], 0.0) for w, row in pairs
        ]
        made += [jnp.zeros((1, SIDE), F32)] * (-len(made) % 8)
        return jnp.concatenate(made, axis=0).T

    def settle(sides):
        items, tails, starts = [], [], {}
        for n in sides:
            flag = (first, last)[n]
            for c in exchanges[n]:
                c.wait_recv()
            rim_rows = slice((0, 66)[n], (2, 68)[n])
            left, _, right = shifts(rim_in[n].astype(F32))
            x3[1, rim_rows] = rim_in[n]
            x3[0, rim_rows] = left.astype(BF16)
            x3[2, rim_rows] = right.astype(BF16)
            starts[n] = [
                start_of(rows_in[n, p, 0], me - 1 if n == 0 else me + 1) + (-SIDE, SIDE)[n] for p in range(SLOTS)
            ]
            pair_first, pair_second = (0, 32)[n], (0, 31)[n]
            static = H_EDGE + 4 + n
            items += [
                (tuple(2 * pair_first + j for j in range(4)), 0),
                (tuple(2 * pair_first + j for j in range(4)), flag),
                ((X_ZERO, 1, 2, X_ZERO) if n == 0 else (65, 66, X_ZERO, X_ZERO), 0),
            ]
            four = tuple(2 * pair_second + j for j in range(4))
            tails += [
                (0, four, 0, (2 * pair_second + 2, 2 * pair_second + 3)),
                (flag, four, flag, (2 * pair_second + 2, 2 * pair_second + 3)),
                (0, (H_ZERO, static, 1, 2), 0, (1, 2)) if n == 0 else (0, (63, 64, static, H_ZERO), 0, (65, 66)),
            ]
            for p in range(SLOTS):
                at = H_EDGE + 6 + 3 * n + p
                if n == 0:
                    e = jnp.clip(starts[n][p] + SIDE - 1, 0, RIM - 1)
                    items.append(((e + 1, e + 2, X_ZERO, X_ZERO), flag))
                    tails.append((flag, (jnp.maximum(e - 1, 0), e, at, H_ZERO), flag, (e + 1, e + 2)))
                else:
                    s = jnp.clip(starts[n][p], RIM, SIDE - 1)
                    items.append(((X_ZERO, s + 2, s + 3, X_ZERO), flag))
                    tails.append((flag, (H_ZERO, at, s + 2, s + 3), flag, (s + 2, s + 3)))

        @stage
        def _():
            made = items_first(items)
            for k, n in enumerate(sides):
                flag, pair_first = (first, last)[n], (0, 32)[n]
                for t in range(3):
                    m = made[t][12 * k : 12 * k + 12]
                    h3[flag, t, 2 * pair_first : 2 * pair_first + 2] = m[2:4]
                    h3[0, t, 2 * pair_first : 2 * pair_first + 2] = m[0:2]
                    h3[0, t, H_EDGE + 4 + n] = m[4]
                    for p in range(SLOTS):
                        h3[flag, t, H_EDGE + 6 + 3 * n + p] = m[6 + 2 * p]

        @stage
        def _():
            result = items_second(tails)
            for k, n in enumerate(sides):
                finish(n, result[6 * k : 6 * k + 6], starts[n])

        for n in sides:
            bulk = pl.ds((2, RIM)[n], RIM - 2)
            late = pltpu.make_async_copy(blend.at[bulk], base_out.at[bulk], out_sem.at[2 + n])
            pl.when((first, last)[n] == 1)(late.start)

    def finish(n, result, starts):
        flag, half, row = (first, last)[n], (0, RIM)[n], (0, SIDE - 2)[n]
        for view, i in ((flag, 1), (0, 0)):
            for q in range(2):
                r_all[view, row + q] = result[i][q]

        near = w_in[n, 0:RIM]
        cover = cov[half : half + RIM] + near
        cov[half : half + RIM] = cover

        pairs, indices = [], [None] * N_ROWS
        for p in range(SLOTS):
            lead = starts[p] + SIDE - 2 if n == 0 else starts[p]
            for q in range(2):
                k = 2 * p + q
                pairs.append((w_in[n, RIM + k : RIM + k + 1], lead + q))
                indices[6 + 6 * n + k] = jnp.where(in_range(lead + q), lead + q, RIM - 2 + 2 * n + q)
        if n == 0:
            pairs += [(own_at(-1, 1), 0), (own_at(0, 0), 0), (own_at(0, 1), 1)]
            for p in range(SLOTS):
                for q in range(2):
                    pairs.append((own_weights[p][q], own_lead[p] + q))
                    indices[2 * p + q] = own_lead[p] + q
        else:
            pairs.append((own_at(1, SIDE - 2), SIDE - 1))
        columns = coefficients(pairs)
        for k in range(6):
            at = 6 + 6 * n + k
            edge[at] = ((result[3 + k // 2][k % 2] - r_all[flag, indices[at]]) * spread(columns, k)).astype(BF16)
        if n == 0:
            for k in range(6):
                edge[k] = ((own_rows[k] - r_all[0, indices[k]]) * spread(columns, 9 + k)).astype(BF16)
        lane = lax.broadcasted_iota(I32, (8, C), 1)
        packed = index[...] if n == 0 else jnp.zeros((8, C), I32)
        for k in range(N_ROWS):
            if indices[k] is not None:
                packed = jnp.where(lane == k, indices[k], packed)
        index[...] = packed

        share = (near / cover).T
        for r in range(half, half + RIM):
            v = r_all[0, r]
            mixed = v + (r_all[1, r] - v) * spread(share, r - half)
            if row <= r < row + 2:
                base[r] = jnp.where(flag == 1, mixed, v).astype(BF16)
            else:
                blend[r] = mixed.astype(BF16)

        def plus(r, v):
            base[r] = (base[r].astype(F32) + v).astype(BF16)

        if n == 0:
            plus(0, (result[2][1] - result[0][0]) * spread(columns, 6)
                 + (own_rows[6] - result[0][0]) * spread(columns, 7))
            plus(1, (own_rows[7] - result[0][1]) * spread(columns, 8))
        else:
            plus(SIDE - 1, (result[2][0] - result[0][1]) * spread(columns, 6))

    @pl.when(me == 0)
    def _():
        settle((1,))
        settle((0,))

    @pl.when(me > 0)
    def _():
        settle((1, 0))

    tail = [
        pltpu.make_async_copy(edge, edge_out, out_sem.at[0]),
        pltpu.make_async_copy(index, index_out, out_sem.at[1]),
        pltpu.make_async_copy(base.at[pl.ds(0, 2)], base_out.at[pl.ds(0, 2)], out_sem.at[4]),
        pltpu.make_async_copy(base.at[pl.ds(SIDE - 2, 2)], base_out.at[pl.ds(SIDE - 2, 2)], out_sem.at[5]),
    ]
    for c in tail:
        c.start()
    writes += tail
    for n in range(2):
        for c in exchanges[n]:
            c.wait_send()
    for c in writes:
        c.wait()


def place(index, base, edge, out, index_s, base_v, edge_v, load_sem, out_sem):
    loads = [
        pltpu.make_async_copy(index, index_s, load_sem.at[0]),
        pltpu.make_async_copy(edge, edge_v, load_sem.at[1]),
    ] + [
        pltpu.make_async_copy(base.at[pl.ds(16 * n, 16)], base_v.at[pl.ds(16 * n, 16)], load_sem.at[2 + n])
        for n in range(4)
    ]
    for c in loads:
        c.start()
    for c in loads:
        c.wait()
    rows = [index_s[0, n] for n in range(N_ROWS)]
    for n in range(0, N_ROWS, 2):
        v = [(base_v[rows[n + q]].astype(F32) + edge_v[n + q].astype(F32)).astype(BF16) for q in range(2)]
        for q in range(2):
            base_v[rows[n + q]] = v[q]
    stores = [
        pltpu.make_async_copy(base_v.at[pl.ds(16 * n, 16)], out.at[pl.ds(16 * n, 16)], out_sem.at[n]) for n in range(4)
    ]
    for c in stores:
        c.start()
    for c in stores:
        c.wait()


def shards(field, patch_rows, flips, blend_weights, live, kernel_one, bias_one, kernel_two, bias_two):
    faces, blks = lax.axis_size("face"), lax.axis_size("blk")
    anywhere = pl.BlockSpec(memory_space=pl.ANY)
    vectors = pl.BlockSpec(memory_space=pltpu.VMEM)
    far = pl.BlockSpec(memory_space=pltpu.HBM)
    base, edge, index = pl.pallas_call(
        functools.partial(work, faces, blks),
        out_shape=(
            jax.ShapeDtypeStruct((SIDE, SIDE, C), BF16),
            jax.ShapeDtypeStruct((N_ROWS, SIDE, C), BF16),
            jax.ShapeDtypeStruct((8, C), I32),
        ),
        in_specs=[anywhere, anywhere, far, anywhere, anywhere, anywhere, vectors, vectors],
        out_specs=(anywhere,) * 3,
        scratch_shapes=[
            pltpu.VMEM((3, X_ZERO + 1, SIDE, C), BF16),
            pltpu.VMEM((2, 3, H_EDGE + N_EDGE, SIDE, C), BF16),
            pltpu.VMEM((2, SIDE, SIDE, C), F32),
            pltpu.VMEM((2, 4, 3, C, 2 * C), BF16),
            pltpu.VMEM((SLOTS, SIDE, SIDE), I32),
            pltpu.VMEM((2, 2, 40, SIDE), F32),
            pltpu.VMEM((2, 40, SIDE), F32),
            pltpu.VMEM((3, 4, SIDE, C), BF16),
            pltpu.VMEM((2, 2, SIDE, C), BF16),
            pltpu.VMEM((2, SLOTS, SIDE), I32),
            pltpu.VMEM((SLOTS, 192, SIDE), F32),
            pltpu.VMEM((SIDE, SIDE), F32),
            pltpu.VMEM((SIDE, SIDE, C), BF16),
            pltpu.VMEM((SIDE, SIDE, C), BF16),
            pltpu.VMEM((8, SIDE, C), F32),
            pltpu.VMEM((N_ROWS, SIDE, C), BF16),
            pltpu.VMEM((8, C), I32),
            pltpu.SMEM((SLOTS, SIDE), I32),
            pltpu.SMEM((1,), I32),
            pltpu.SemaphoreType.DMA((4,)),
            pltpu.SemaphoreType.DMA((9,)),
            pltpu.SemaphoreType.DMA((2, 3)),
            pltpu.SemaphoreType.DMA((2, 3)),
            pltpu.SemaphoreType.DMA((6,)),
        ],
        compiler_params=pltpu.CompilerParams(
            collective_id=0, has_side_effects=True, vmem_limit_bytes=62 * 2**20
        ),
    )(
        field, patch_rows, live, blend_weights, kernel_one, kernel_two,
        bias_one.reshape(1, C), bias_two.reshape(1, C),
    )
    return pl.pallas_call(
        place,
        out_shape=jax.ShapeDtypeStruct((SIDE, SIDE, C), BF16),
        in_specs=[anywhere] * 3,
        out_specs=anywhere,
        scratch_shapes=[
            pltpu.SMEM((8, C), I32),
            pltpu.VMEM((SIDE, SIDE, C), BF16),
            pltpu.VMEM((N_ROWS, SIDE, C), BF16),
            pltpu.SemaphoreType.DMA((6,)),
            pltpu.SemaphoreType.DMA((4,)),
        ],
        compiler_params=pltpu.CompilerParams(vmem_limit_bytes=62 * 2**20),
    )(index, base, edge)


def solution(mesh):
    split = ("face", "blk")
    placed = (P(split, None, None), P(split, None), P(split, None), P(split, None, None), P(split), P(), P(), P(), P())
    return jax.shard_map(shards, mesh=mesh, in_specs=placed, out_specs=P(split, None, None), check_vma=False)
```

time: 20.3 us -> 18.6 us (0.916)
  the two profiles are of different devices: /device:TPU:127 before, /device:TPU:0 now
where the time goes in v1:
time: 18.6 us; the launch traced here: 18.4 us
  Pallas kernels  17.7 us (95%)
  between operations  0.66 us (4%)
    pallas_call x1, Pallas kernels, shards(): pl.pallas_call(functools.partial(work, faces, blks), out_shape=(jax.Shape...  15.3 us
    pallas_call x1, Pallas kernels, shards(): pl.pallas_call(place, out_shape=jax.ShapeDtypeStruct((SIDE, SIDE, C), BF1...  2.41 us

profile of v1, /device:TPU:0, one launch (start us, length us, event | category | flops | bytes accessed | tf_op | source)
XLA Modules:
  0.0 18.4 jit_solution(2262445525414084558)
XLA Ops:
  0.7 15.3 %shard_map.82 = (bf16[64,64,128]{2,1,0:T(8,128)(2,1)}, bf16[18,64,128]{2,1,0:T(8,128)(2,1)}, s32[8,128]{1,0:T(8,128)}) custom-call(bf16[64,64,128]{2,1,0:T(8,128)(2,1)} %field.1, s32[3,64]{1,0:T(4,128)} %rows.1, s32[1]{0:T(128)S(6)} %copy.9.live, s32[3,64,64]{2,1,0:T(8,128)} %weights.1, bf16[3,3,128,128]{3,2,1,0:T(8,128)(2,1)} %k_one.1, ...), custom_call_target="tpu_custom_call" | custom-call | tf_op jit(solution)/shard_map/pallas_call | solution.py:512
  16.0 2.4 %shard_map.83 = bf16[64,64,128]{2,1,0:T(8,128)(2,1)} custom-call(s32[8,128]{1,0:T(8,128)} %get-tuple-element.8.index, bf16[64,64,128]{2,1,0:T(8,128)(2,1)} %get-tuple-element.9.base, bf16[18,64,128]{2,1,0:T(8,128)(2,1)} %get-tuple-element.10.edge), custom_call_target="tpu_custom_call" | custom-call | tf_op jit(solution)/shard_map/pallas_call | solution.py:554

commit v2 on v1

--- a/solution.py
+++ b/solution.py
@@ -54,7 +54,7 @@
     field, rows, live, weights, k_one, k_two, b_one, b_two,
     base_out, edge_out, index_out,
     x3, h3, r_all, wmat, wts, w_send, w_in, rim, rim_in, rows_in, wown, cov, base, blend, own_rows, edge, index,
-    rows_s, live_s,
+    bias, rows_s, live_s,
     field_sem, load_sem, send_sem, recv_sem, out_sem,
 ):
     me_face, me_blk = lax.axis_index("face"), lax.axis_index("blk")
@@ -90,8 +90,18 @@
         )
         for conv, src in enumerate((k_one, k_two)) for q in range(2)
     ]
-    for c in small_loads + field_loads[:1] + kernel_loads[:2] + field_loads[1:] + kernel_loads[2:]:
-        c.start()
+    bias_loads = [
+        pltpu.make_async_copy(src, bias.at[conv], load_sem.at[9 + conv]) for conv, src in enumerate((b_one, b_two))
+    ]
+    early = field_loads[:1] + kernel_loads[:2] + bias_loads[:1]
+
+    def start(copies):
+        for c in copies:
+            c.start()
+
+    pl.when(me_blk == blks - 1)(lambda: start(small_loads + early))
+    pl.when(me_blk < blks - 1)(lambda: start(early + small_loads))
+    start(field_loads[1:] + kernel_loads[2:] + bias_loads[1:])
 
     for conv in range(2):
         wmat[conv, 0, :, :, C:] = jnp.zeros((3, C, C), BF16)
@@ -160,12 +170,10 @@
             for t in range(3)
         ]
 
-    bias_one = b_one[...]
-    bias_two = b_two[...]
 
     def hidden_of(acc):
         h = unpair(acc)
-        h = silu(h.reshape(-1, SIDE, C) + bias_one.reshape(1, 1, C))
+        h = silu(h.reshape(-1, SIDE, C) + bias[0].reshape(1, 1, C))
         return [v.astype(BF16) for v in shifts(h)]
 
     def first_conv(view, first_row, pairs, mirrored):
@@ -175,7 +183,7 @@
 
     def second_conv(view, pair, pairs, mirrored):
         acc = pair_dot(run_parts(h3.at[view], 2 * pair, pairs, mirrored), wmat, 1)
-        r = unpair(acc).reshape(2 * pairs, SIDE, C) + bias_two.reshape(1, 1, C)
+        r = unpair(acc).reshape(2 * pairs, SIDE, C) + bias[1].reshape(1, 1, C)
         r = r + x3[1, pl.ds(2 + 2 * pair, 2 * pairs)].astype(F32)
         r_all[view, pl.ds(2 * pair, 2 * pairs)] = r
         if view == 0:
@@ -190,7 +198,7 @@
 
     field_loads[0].wait()
     shift_field(2, 16)
-    for c in kernel_loads[:2]:
+    for c in kernel_loads[:2] + bias_loads[:1]:
         c.wait()
     first_conv(0, 2, 7, False)
 
@@ -215,7 +223,7 @@
         first_conv(0, 32, 8, False)
         first_conv(0, 48, 8, False)
 
-    for c in kernel_loads[2:]:
+    for c in kernel_loads[2:] + bias_loads[1:]:
         c.wait()
 
     @stage
@@ -273,7 +281,7 @@
             )
             for t in range(3)
         ]
-        r = unpair(pair_dot(parts, wmat, 1)) + bias_two.reshape(1, 1, 1, C)
+        r = unpair(pair_dot(parts, wmat, 1)) + bias[1].reshape(1, 1, 1, C)
         return [
             [r[n, q] + x3[1, residual[q]].astype(F32) for q in range(2)]
             for n, (_, _, _, residual) in enumerate(items)
@@ -507,8 +515,6 @@
 def shards(field, patch_rows, flips, blend_weights, live, kernel_one, bias_one, kernel_two, bias_two):
     faces, blks = lax.axis_size("face"), lax.axis_size("blk")
     anywhere = pl.BlockSpec(memory_space=pl.ANY)
-    vectors = pl.BlockSpec(memory_space=pltpu.VMEM)
-    far = pl.BlockSpec(memory_space=pltpu.HBM)
     base, edge, index = pl.pallas_call(
         functools.partial(work, faces, blks),
         out_shape=(
@@ -516,7 +522,7 @@
             jax.ShapeDtypeStruct((N_ROWS, SIDE, C), BF16),
             jax.ShapeDtypeStruct((8, C), I32),
         ),
-        in_specs=[anywhere, anywhere, far, anywhere, anywhere, anywhere, vectors, vectors],
+        in_specs=[anywhere] * 8,
         out_specs=(anywhere,) * 3,
         scratch_shapes=[
             pltpu.VMEM((3, X_ZERO + 1, SIDE, C), BF16),
@@ -536,10 +542,11 @@
             pltpu.VMEM((8, SIDE, C), F32),
             pltpu.VMEM((N_ROWS, SIDE, C), BF16),
             pltpu.VMEM((8, C), I32),
+            pltpu.VMEM((2, 1, C), F32),
             pltpu.SMEM((SLOTS, SIDE), I32),
             pltpu.SMEM((1,), I32),
             pltpu.SemaphoreType.DMA((4,)),
-            pltpu.SemaphoreType.DMA((9,)),
+            pltpu.SemaphoreType.DMA((11,)),
             pltpu.SemaphoreType.DMA((2, 3)),
             pltpu.SemaphoreType.DMA((2, 3)),
             pltpu.SemaphoreType.DMA((6,)),

time: 18.6 us -> 17.9 us (0.962)
  Pallas kernels: 17.7 us -> 17.1 us
    pallas_call x1, Pallas kernels: 15.3 us -> 14.7 us  [shards(): pl.pallas_call(functools.partial(work, faces, blks), out_shape=(jax.Shape...]
where the time goes in v2:
time: 17.9 us; the launch traced here: 17.8 us
  Pallas kernels  17.1 us (96%)
  between operations  0.66 us (4%)
    pallas_call x1, Pallas kernels, shards(): pl.pallas_call(functools.partial(work, faces, blks), out_shape=(jax.Shape...  14.7 us
    pallas_call x1, Pallas kernels, shards(): pl.pallas_call(place, out_shape=jax.ShapeDtypeStruct((SIDE, SIDE, C), BF1...  2.41 us

profile of v2, /device:TPU:0, one launch (start us, length us, event | category | flops | bytes accessed | tf_op | source)
XLA Modules:
  0.0 17.8 jit_solution(1312621465724848642)
XLA Ops:
  0.7 14.7 %shard_map.82 = (bf16[64,64,128]{2,1,0:T(8,128)(2,1)}, bf16[18,64,128]{2,1,0:T(8,128)(2,1)}, s32[8,128]{1,0:T(8,128)}) custom-call(bf16[64,64,128]{2,1,0:T(8,128)(2,1)} %field.1, s32[3,64]{1,0:T(4,128)} %rows.1, s32[1]{0:T(128)S(6)} %copy.9.live, s32[3,64,64]{2,1,0:T(8,128)} %weights.1, bf16[3,3,128,128]{3,2,1,0:T(8,128)(2,1)} %k_one.1, ...), custom_call_target="tpu_custom_call" | custom-call | tf_op jit(solution)/shard_map/pallas_call | solution.py:518
  15.4 2.4 %shard_map.83 = bf16[64,64,128]{2,1,0:T(8,128)(2,1)} custom-call(s32[8,128]{1,0:T(8,128)} %get-tuple-element.8.index, bf16[64,64,128]{2,1,0:T(8,128)(2,1)} %get-tuple-element.9.base, bf16[18,64,128]{2,1,0:T(8,128)(2,1)} %get-tuple-element.10.edge), custom_call_target="tpu_custom_call" | custom-call | tf_op jit(solution)/shard_map/pallas_call | solution.py:561

commit v3 on v2

--- a/solution.py
+++ b/solution.py
@@ -246,13 +246,13 @@
         first_conv(1, 2 * (1 + b), 8, True)
         first_conv(1, 2 * (9 + b), 8, True)
 
-    pl.when(me == 0)(lambda: send(1))
-
     @pl.when(boundary)
     def _():
         b = jnp.where(me_blk == 0, 0, 15)
         second_conv(1, 1 + b, 8, True)
         second_conv(1, 9 + b, 7, True)
+
+    pl.when(me == 0)(lambda: send(1))
 
     own_starts = [start_of(rows_s[p, 0], me) for p in range(SLOTS)]
 
@@ -461,12 +461,12 @@
         else:
             plus(SIDE - 1, (result[2][0] - result[0][1]) * spread(columns, 6))
 
-    @pl.when(me == 0)
+    @pl.when(me <= 1)
     def _():
         settle((1,))
         settle((0,))
 
-    @pl.when(me > 0)
+    @pl.when(me > 1)
     def _():
         settle((1, 0))
 

time: 17.9 us -> 17.5 us (0.978)
  Pallas kernels: 17.1 us -> 16.7 us
    pallas_call x1, Pallas kernels: 14.7 us -> 14.2 us  [shards(): pl.pallas_call(functools.partial(work, faces, blks), out_shape=(jax.Shape...]
where the time goes in v3:
time: 17.5 us; the launch traced here: 17.3 us
  Pallas kernels  16.7 us (95%)
  between operations  0.66 us (4%)
    pallas_call x1, Pallas kernels, shards(): pl.pallas_call(functools.partial(work, faces, blks), out_shape=(jax.Shape...  14.2 us
    pallas_call x1, Pallas kernels, shards(): pl.pallas_call(place, out_shape=jax.ShapeDtypeStruct((SIDE, SIDE, C), BF1...  2.41 us

profile of v3, /device:TPU:0, one launch (start us, length us, event | category | flops | bytes accessed | tf_op | source)
XLA Modules:
  0.0 17.3 jit_solution(15781971614900175979)
XLA Ops:
  0.7 14.2 %shard_map.82 = (bf16[64,64,128]{2,1,0:T(8,128)(2,1)}, bf16[18,64,128]{2,1,0:T(8,128)(2,1)}, s32[8,128]{1,0:T(8,128)}) custom-call(bf16[64,64,128]{2,1,0:T(8,128)(2,1)} %field.1, s32[3,64]{1,0:T(4,128)} %rows.1, s32[1]{0:T(128)S(6)} %copy.9.live, s32[3,64,64]{2,1,0:T(8,128)} %weights.1, bf16[3,3,128,128]{3,2,1,0:T(8,128)(2,1)} %k_one.1, ...), custom_call_target="tpu_custom_call" | custom-call | tf_op jit(solution)/shard_map/pallas_call | solution.py:518
  14.9 2.4 %shard_map.83 = bf16[64,64,128]{2,1,0:T(8,128)(2,1)} custom-call(s32[8,128]{1,0:T(8,128)} %get-tuple-element.8.index, bf16[64,64,128]{2,1,0:T(8,128)(2,1)} %get-tuple-element.9.base, bf16[18,64,128]{2,1,0:T(8,128)(2,1)} %get-tuple-element.10.edge), custom_call_target="tpu_custom_call" | custom-call | tf_op jit(solution)/shard_map/pallas_call | solution.py:561
